TPU v7x, 32 devices: a whole 2x2x4 slice. The times are simulated.
32 devices in a mesh: rec: 4 (over y, core), tract: 8 (over z, x).
Axes of the slice: x: 2, y: 2, z: 4, core: 2. Of those that a mesh axis runs over, the one named last changes fastest.
Arguments:
- rep_weights: float32 [80, 131072], P(None, ('rec', 'tract')), may hold values from 0.5 to 2
- covariate_codes: int32 [5, 131072], P(None, ('rec', 'tract')), may hold values from 0 to 15
- tract_of: int32 [131072, 1], P(('rec', 'tract')), may hold values from 0 to 7; in each aligned block of 4096 rows (0 to 4095, 4096 to 8191, ...) at most 1536 rows name the same one
- log_income: bfloat16 [131072], P(('rec', 'tract')), may hold values from -5 to 5
- controls: float32 [64], replicated, may hold values from 7782 to 10240
- threshold_grid: int32 [2048], replicated, may hold values from 0 to 4095
Outputs:
- calibrated: float32 [80, 131072], P(None, ('rec', 'tract'))
- income_tables: float32 [8, 80, 2048], P('tract', None, 'rec')
Inputs may be any that keep to these rules, and one draw needn't show every extreme that they name: `tract_of`: among the 4096 persons of one device at most 1536 share a tract; in some aligned blocks of 4096 persons one tract has exactly 1536.
All inputs are finite; a program needn't handle non-finite values.
Results may differ from a plain program's by a relative error of at most 0.0003.
Values may be sent and summed in bfloat16 or wider, within the bound.
A program may use at most 128 MiB of HBM per device.

v0:
```python
import math
import jax
import jax.numpy as jnp
from jax import lax
from jax.sharding import PartitionSpec as P

smooth_width = 3.0 / 8192.0
grid_middle = 2048.0
grid_step = 3.0 / 2048.0
base_levels = 16
first_kept = 4


def design(covariate_codes):
    level_codes = jnp.arange(base_levels, dtype=jnp.int32)
    kept_levels = jnp.arange(first_kept, base_levels, dtype=jnp.int32)
    groups = [covariate_codes[0][None, :] == level_codes[:, None]]
    for variable in range(1, covariate_codes.shape[0]):
        groups.append(covariate_codes[variable][None, :] == kept_levels[:, None])
    return jnp.concatenate(groups, axis=0).astype(jnp.float32)


def solve_controls(gram_sums, totals, controls):
    factor = jnp.linalg.cholesky(gram_sums)
    gap = (controls[None, :] - totals)[:, :, None]
    middle = lax.linalg.triangular_solve(factor, gap, left_side=True, lower=True)
    result = lax.linalg.triangular_solve(
        factor, middle, left_side=True, lower=True, transpose_a=True
    )
    return result[:, :, 0]


def shards(rep_weights, covariate_codes, tract_of, log_income, controls, threshold_grid):
    rep_count, row_count = rep_weights.shape
    ctrl_count = controls.shape[0]
    tract_count = lax.axis_size("tract")
    rec_count = lax.axis_size("rec")
    design_rows = design(covariate_codes)
    block_rows = math.gcd(row_count, 256)

    def gram_step(position, running):
        weight_block = lax.dynamic_slice_in_dim(rep_weights, position * block_rows, block_rows, 1)
        design_block = lax.dynamic_slice_in_dim(design_rows, position * block_rows, block_rows, 1)
        spread = (weight_block[:, None, :] * design_block[None, :, :]).reshape(
            rep_count * ctrl_count, block_rows
        )
        product = jnp.einsum("an,cn->ac", spread, design_block, precision=lax.Precision.HIGHEST)
        return running + product.reshape(rep_count, ctrl_count, ctrl_count)

    gram_sums = lax.fori_loop(
        0,
        row_count // block_rows,
        gram_step,
        jnp.zeros((rep_count, ctrl_count, ctrl_count), jnp.float32),
    )
    totals = jnp.einsum("rn,cn->rc", rep_weights, design_rows, precision=lax.Precision.HIGHEST)
    gram_sums, totals = lax.psum((gram_sums, totals), ("rec", "tract"))
    multipliers = solve_controls(gram_sums, totals, controls)
    factors = 1.0 + jnp.dot(multipliers, design_rows, precision=lax.Precision.HIGHEST)
    calibrated = rep_weights * factors
    sent_weights = calibrated.astype(jnp.bfloat16)
    centers = (threshold_grid.astype(jnp.float32) - grid_middle) * grid_step
    tract_ids = tract_of[:, 0]
    per_tract = float(row_count * rec_count)
    capacity = 3 * row_count // tract_count
    belongs = (tract_ids[:, None] == jnp.arange(tract_count, dtype=jnp.int32)[None, :]).astype(
        jnp.int32
    )
    earlier = jnp.cumsum(belongs, axis=0) - belongs
    slot_index = jnp.sum(earlier * belongs, axis=1)
    target = tract_ids * capacity + slot_index
    source = jnp.full((tract_count * capacity,), row_count, jnp.int32)
    source = source.at[target].set(jnp.arange(row_count, dtype=jnp.int32))
    payload = jnp.concatenate([sent_weights, log_income[None, :]], axis=0)
    payload = jnp.concatenate([payload, jnp.zeros((rep_count + 1, 1), jnp.bfloat16)], axis=1)
    buffer = jnp.take(payload, source.reshape(tract_count, capacity), axis=1)
    received = lax.all_to_all(buffer, "tract", split_axis=1, concat_axis=1, tiled=True)
    recv_weights = received[:rep_count]
    recv_income = received[rep_count].astype(jnp.float32)
    smoothed = jax.nn.sigmoid((centers[None, None, :] - recv_income[:, :, None]) / smooth_width)
    smoothed = smoothed.astype(jnp.bfloat16)
    term = lax.psum_scatter(
        jnp.einsum("rsm,smj->jr", recv_weights, smoothed, preferred_element_type=jnp.float32),
        "rec",
        scatter_dimension=0,
        tiled=True,
    )
    income_tables = (term.T / per_tract)[None]
    return (calibrated, income_tables)


def solution(mesh):
    placed = (
        P(None, ("rec", "tract")),
        P(None, ("rec", "tract")),
        P(("rec", "tract"), None),
        P(("rec", "tract")),
        P(),
        P(),
    )
    return jax.shard_map(
        shards,
        mesh=mesh,
        in_specs=placed,
        out_specs=(P(None, ("rec", "tract")), P("tract", None, "rec")),
        check_vma=False,
    )
```

profile of v0, /device:TPU:0, one launch (start us, length us, event | category | flops | bytes accessed | tf_op | source)
XLA Modules:
  0.0 996.2 jit_solution(17329571507120278312)
XLA Ops:
  7.2 1.5 fusion.21
  9.0 13.0 %concatenate.9 = pred[64,4096]{1,0:T(32,128)(4,1)S(1)} concatenate(pred[16,4096]{1,0:T(8,128)(4,1)S(1)} %iota_compare_fusion, pred[12,4096]{1,0:T(8,128)(4,1)S(1)} %get-tuple-element.113, pred[12,4096]{1,0:T(8,128)(4,1)S(1)} %get-tuple-element.111, pred[12,4096]{1,0:T(8,128)(4,1)S(1)} %get-tuple-element.112, pred[12,4096]{1,0:T(8,128)(4,1)S(1)} %get-tuple-element.110), dimensions={0} | concatenate | bytes 524288 | tf_op jit(solution)/shard_map/concatenate | solution.py:20
  22.0 1.1 convert_element_type.29
  23.1 109.5 %while.14 = (s32[]{:T(128)}, f32[80,64,64]{2,1,0:T(8,128)S(1)}, f32[80,4096]{1,0:T(8,128)}, f32[64,4096]{1,0:T(8,128)}, s32[]{:T(128)}, /*index=5*/s32[]{:T(128)}, s32[]{:T(128)}, s32[]{:T(128)}) while((s32[]{:T(128)}, f32[80,64,64]{2,1,0:T(8,128)S(1)}, f32[80,4096]{1,0:T(8,128)}, f32[64,4096]{1,0:T(8,128)}, s32[]{:T(128)}, ...), condition=%wide.region_1.0_spmd.clone, body=%wide.region_0.0_spmd.clone.sunk | while | flops 1008599040 | bytes 3063957 | solution.py:50
  24.9 5.1 select_add_fusion.2
  30.0 0.9 constant_dynamic-slice_fusion.5
  31.7 5.1 select_add_fusion.2
  36.8 0.9 constant_dynamic-slice_fusion.5
  38.6 5.1 select_add_fusion.2
  43.7 0.9 constant_dynamic-slice_fusion.5
  45.4 5.1 select_add_fusion.2
  52.3 5.1 select_add_fusion.2
  57.4 0.9 constant_dynamic-slice_fusion.5
  59.1 5.1 select_add_fusion.2
  66.0 5.1 select_add_fusion.2
  72.8 5.1 select_add_fusion.2
  79.7 5.1 select_add_fusion.2
  86.5 5.1 select_add_fusion.2
  93.4 5.1 select_add_fusion.2
  100.2 5.1 select_add_fusion.2
  107.0 5.1 select_add_fusion.2
  113.9 5.1 select_add_fusion.2
  120.7 5.1 select_add_fusion.2
  127.6 5.1 select_add_fusion.2
  132.7 2.1 copy.20
  134.9 1.2 copy-done.2
  137.0 2.3 reduce-window.6
  140.1 15.5 %scatter_custom_fusion = s32[12288]{0:T(1024)S(1)} fusion(s32[4096]{0:T(1024)S(1)} %bitcast.84, s32[4096]{0:T(1024)S(1)} %iota.52, s32[]{:T(128)} %constant.113.clone.1), kind=kCustom, calls=%fused_computation.50 | custom fusion | bytes 49156 | tf_op jit(solution)/shard_map/scatter | solution.py:73
  155.6 42.5 %psum.15 = f32[80,64]{0,1:T(8,128)S(1)} all-reduce(f32[80,64]{0,1:T(8,128)S(1)} %convolution_bitcast_fusion), channel_id=1, replica_groups=mesh['rec'=4,'tract'=8] {'rec','tract'}, use_global_device_ids=true, to_apply=%region_5.6 | all-reduce | flops 5120 | bytes 40960 | tf_op jit(solution)/shard_map/psum | solution.py:57
  198.3 75.6 %all-reduce.3.cloned.1.call-done = f32[80,64,64]{1,2,0:T(8,128)} async-done(((f32[80,64,64]{1,2,0:T(8,128)}), f32[80,64,64]{1,2,0:T(8,128)}) %all-reduce.3.cloned.1.call-update) | async-done | bytes 1310736 | tf_op jit(solution)/shard_map/psum | solution.py:57
  273.9 3.4 copy.21
  277.3 3.8 fusion.9
  281.1 470.7 %custom-call.9 = f32[80,64,64]{2,1,0:T(8,128)} custom-call(f32[80,64,64]{2,1,0:T(8,128)} %fusion.9), custom_call_target="Cholesky" | custom-call | tf_op jit(solution)/shard_map/jit(cholesky)/cholesky | solution.py:24
  751.8 2.7 copy.22
  755.3 1.7 select_bitcast_fusion.1
  757.0 67.2 %custom-call.10 = f32[80,1,64,64]{0,2,3,1:T(8,128)S(1)} custom-call(f32[80,1,64,64]{0,3,2,1:T(8,128)} %select_bitcast_fusion.1), custom_call_target="InvertDiagBlocksLowerTriangular" | custom-call | tf_op jit(solution)/shard_map/triangular_solve | solution.py:27
  824.6 1.0 copy-done.1
  825.6 3.6 copy.33
  829.2 4.2 fusion.23
  833.4 1.8 fusion.22
  836.2 43.3 %gather_fusion = bf16[12288,81]{1,0:T(8,128)(2,1)} fusion(bf16[81,4097]{0,1:T(8,128)(2,1)S(1)} %concatenate.11.clone, s32[12288]{0:T(1024)S(1)} %broadcast_clamp_fusion), kind=kCustom, calls=%fused_computation | custom fusion | bytes 4030464 | tf_op jit(solution)/shard_map/jit(_take)/gather | solution.py:76
  879.5 3.3 copy.26
  882.8 1.6 select_bitcast_fusion
  884.4 4.0 all-to-all-start
  888.5 48.2 %all-to-all-done = bf16[81,8,1536]{2,0,1:T(8,128)(2,1)S(1)} async-done(((bf16[81,8,1536]{2,0,1:T(8,128)(2,1)}), bf16[81,8,1536]{2,0,1:T(8,128)(2,1)S(1)}, u32[]{:S(2)}, u32[]{:S(2)}) %all-to-all-start) | async-done | bytes 1990688 | tf_op jit(solution)/shard_map/all_to_all | solution.py:77
  936.7 29.7 %fusion.10 = f32[2048,80]{0,1:T(8,128)} fusion(f32[8,1536]{1,0:T(8,128)S(1)} %bitcast.82, f32[2048]{0:T(1024)S(1)} %add_multiply_fusion, bf16[81,8,1536]{2,0,1:T(8,128)(2,1)S(1)} %all-to-all-done), kind=kOutput, calls=%fused_computation.16 | convolution fusion | flops 4177526784 | bytes 2678784 | tf_op jit(solution)/shard_map/rsm,smj->jr/dot_general | solution.py:83
  966.4 21.3 %reduce-scatter.2.cloned.1.call-done = f32[512,80]{0,1:T(8,128)} async-done(((f32[2048,80]{0,1:T(8,128)}), f32[512,80]{0,1:T(8,128)}) %reduce-scatter.2.cloned.1.call-update) | async-done | bytes 163856 | tf_op jit(solution)/shard_map/reduce_scatter | solution.py:82
  987.8 1.6 multiply_bitcast_fusion
  (78 shorter events, 28.5 us)
Async XLA Ops:
  7.2 266.7 %all-reduce.3.cloned.1.call-start = ((), (), s32[]{:S(2)}) async-start(), calls=%async_computation.2 | async-start | bytes 5242880 | tf_op jit(solution)/shard_map/psum | solution.py:57
  134.8 1.3 copy-start.2
  134.8 2.1 copy-start.4
  134.8 63.3 %copy-start.5 = (bf16[4096]{0:T(1024)(128)(2,1)S(1)}, bf16[4096]{0:T(1024)(128)(2,1)}, u32[]{:S(2)}) copy-start(bf16[4096]{0:T(1024)(128)(2,1)} %param.11) | copy-start | bytes 24580
  134.8 63.4 %copy-start.7 = (f32[64]{0:T(128)S(1)}, f32[64]{0:T(128)}, u32[]{:S(2)}) copy-start(f32[64]{0:T(128)} %param.12) | copy-start | bytes 772
  273.9 3.4 copy-start
  824.3 1.4 copy-start.1
  829.2 4.2 copy-start.3
  884.4 4.1 copy-start.6
  884.4 52.3 %all-to-all-start = ((bf16[81,8,1536]{2,0,1:T(8,128)(2,1)}), bf16[81,8,1536]{2,0,1:T(8,128)(2,1)S(1)}, u32[]{:S(2)}, u32[]{:S(2)}) async-start(bf16[81,8,1536]{2,0,1:T(8,128)(2,1)} %select_bitcast_fusion), calls=%async_computation | async-start | bytes 4325376 | tf_op jit(solution)/shard_map/all_to_all | solution.py:77
  888.4 99.3 %reduce-scatter.2.cloned.1.call-start = ((), (), s32[]{:S(2)}) async-start(), calls=%async_computation.3 | async-start | bytes 819200 | tf_op jit(solution)/shard_map/reduce_scatter | solution.py:82
Sparse Core Ops, SparseCore 0:
  135.0 138.9 all-reduce.2
  966.5 21.1 reduce-scatter.1
where the time goes:
time: 998 us; the launch traced here: 996 us
  other arithmetic  552 us (55%)
  waiting for transfers between devices  145 us (15%)
  local copies, waits for them, and re-layouts  120 us (12%)
  matrix products  118 us (12%)
  blocking collectives  42.5 us (4%)
  between operations  14.4 us (1%)
    another operation x4, other arithmetic, solve_controls(): factor = jnp.linalg.cholesky(gram_sums)  471 us
    dot_general x16, matrix products, gram_step(): jnp.einsum('an,cn->ac', spread, design_block, precision=lax.Precision.HIG...  81.2 us
    psum x1, waiting for transfers between devices, shards(): gram_sums, totals = lax.psum((gram_sums, totals), ('rec', 'tract'))  75.6 us
    another operation x3, other arithmetic, solve_controls(): lax.linalg.triangular_solve(factor, middle, left_side=True, lower=True, t...  69 us
    all_to_all x1, waiting for transfers between devices, shards(): lax.all_to_all(buffer, 'tract', split_axis=1, concat_axis=1, tiled=True)  48.2 us
    gather x2, local copies, waits for them, and re-layouts, shards(): buffer = jnp.take(payload, source.reshape(tract_count, capacity), axis=1)  46.6 us
    psum x1, blocking collectives, shards(): gram_sums, totals = lax.psum((gram_sums, totals), ('rec', 'tract'))  42.5 us
    dot_general x1, matrix products, shards(): jnp.einsum('rsm,smj->jr', recv_weights, smoothed, preferred_element_type=...  29.7 us
  transfers between devices with their start and end apart: 3, of which 3 were waited for; matrix products, arithmetic and copies ran while one was open for 2% of the time, Pallas kernels for 0%

commit v1 on v0

--- a/solution.py
+++ b/solution.py
@@ -54,7 +54,7 @@
         jnp.zeros((rep_count, ctrl_count, ctrl_count), jnp.float32),
     )
     totals = jnp.einsum("rn,cn->rc", rep_weights, design_rows, precision=lax.Precision.HIGHEST)
-    gram_sums, totals = lax.psum((gram_sums, totals), ("rec", "tract"))
+    gram_sums, totals = lax.psum(lax.psum((gram_sums, totals), "tract"), "rec")
     multipliers = solve_controls(gram_sums, totals, controls)
     factors = 1.0 + jnp.dot(multipliers, design_rows, precision=lax.Precision.HIGHEST)
     calibrated = rep_weights * factors

time: 998 us -> 1040 us (1.042)
  waiting for transfers between devices: 145 us -> 181 us
    psum x1 -> x2, waiting for transfers between devices: 75.6 us -> 110 us  [shards(): gram_sums, totals = lax.psum(lax.psum((gram_sums, totals), 'tract'), 'rec')]
    psum x1 -> x2, blocking collectives: 42.5 us -> 50.1 us  [shards(): gram_sums, totals = lax.psum(lax.psum((gram_sums, totals), 'tract'), 'rec')]
  transfers between devices with their start and end apart: 3 -> 4, of which waited for: 3 -> 4; matrix products, arithmetic and copies ran while one was open for 2% -> 2% of each run, Pallas kernels for 0% -> 0%
where the time goes in v1:
time: 1040 us
  other arithmetic  552 us (53%)
  waiting for transfers between devices  181 us (17%)
  local copies, waits for them, and re-layouts  119 us (11%)
  matrix products  118 us (11%)
  blocking collectives  50.1 us (5%)
  between operations  14.1 us (1%)
    another operation x4, other arithmetic, solve_controls(): factor = jnp.linalg.cholesky(gram_sums)  471 us
    psum x2, waiting for transfers between devices, shards(): gram_sums, totals = lax.psum(lax.psum((gram_sums, totals), 'tract'), 'rec')  110 us
    dot_general x16, matrix products, gram_step(): jnp.einsum('an,cn->ac', spread, design_block, precision=lax.Precision.HIG...  81.2 us
    another operation x3, other arithmetic, solve_controls(): lax.linalg.triangular_solve(factor, middle, left_side=True, lower=True, t...  69 us
    psum x2, blocking collectives, shards(): gram_sums, totals = lax.psum(lax.psum((gram_sums, totals), 'tract'), 'rec')  50.1 us
    all_to_all x1, waiting for transfers between devices, shards(): lax.all_to_all(buffer, 'tract', split_axis=1, concat_axis=1, tiled=True)  49.5 us
    gather x2, local copies, waits for them, and re-layouts, shards(): buffer = jnp.take(payload, source.reshape(tract_count, capacity), axis=1)  46.6 us
    dot_general x1, matrix products, shards(): jnp.einsum('rsm,smj->jr', recv_weights, smoothed, preferred_element_type=...  29.7 us
  transfers between devices with their start and end apart: 4, of which 4 were waited for; matrix products, arithmetic and copies ran while one was open for 2% of the time, Pallas kernels for 0%

profile of v1, /device:TPU:0, one launch (start us, length us, event | category | flops | bytes accessed | tf_op | source)
XLA Modules:
  0.0 1040.1 jit_solution(11303547499726919429)
XLA Ops:
  7.2 1.5 fusion.21
  9.0 13.0 %concatenate.9 = pred[64,4096]{1,0:T(32,128)(4,1)S(1)} concatenate(pred[16,4096]{1,0:T(8,128)(4,1)S(1)} %iota_compare_fusion, pred[12,4096]{1,0:T(8,128)(4,1)S(1)} %get-tuple-element.113, pred[12,4096]{1,0:T(8,128)(4,1)S(1)} %get-tuple-element.111, pred[12,4096]{1,0:T(8,128)(4,1)S(1)} %get-tuple-element.112, pred[12,4096]{1,0:T(8,128)(4,1)S(1)} %get-tuple-element.110), dimensions={0} | concatenate | bytes 524288 | tf_op jit(solution)/shard_map/concatenate | solution.py:20
  22.0 1.1 convert_element_type.29
  23.1 109.5 %while.14 = (s32[]{:T(128)}, f32[80,64,64]{2,1,0:T(8,128)S(1)}, f32[80,4096]{1,0:T(8,128)}, f32[64,4096]{1,0:T(8,128)}, s32[]{:T(128)}, /*index=5*/s32[]{:T(128)}, s32[]{:T(128)}, s32[]{:T(128)}) while((s32[]{:T(128)}, f32[80,64,64]{2,1,0:T(8,128)S(1)}, f32[80,4096]{1,0:T(8,128)}, f32[64,4096]{1,0:T(8,128)}, s32[]{:T(128)}, ...), condition=%wide.region_1.0_spmd.clone, body=%wide.region_0.0_spmd.clone.sunk | while | flops 1008599040 | bytes 3063957 | solution.py:50
  24.9 5.1 select_add_fusion.2
  30.0 0.9 constant_dynamic-slice_fusion.5
  31.7 5.1 select_add_fusion.2
  36.8 0.9 constant_dynamic-slice_fusion.5
  38.6 5.1 select_add_fusion.2
  45.4 5.1 select_add_fusion.2
  52.3 5.1 select_add_fusion.2
  57.4 0.9 constant_dynamic-slice_fusion.5
  59.1 5.1 select_add_fusion.2
  66.0 5.1 select_add_fusion.2
  72.8 5.1 select_add_fusion.2
  79.7 5.1 select_add_fusion.2
  86.5 5.1 select_add_fusion.2
  93.4 5.1 select_add_fusion.2
  100.2 5.1 select_add_fusion.2
  107.0 5.1 select_add_fusion.2
  113.9 5.1 select_add_fusion.2
  120.7 5.1 select_add_fusion.2
  127.6 5.1 select_add_fusion.2
  132.7 2.1 copy.20
  135.5 2.3 reduce-window.6
  138.6 15.5 %scatter_custom_fusion = s32[12288]{0:T(1024)S(1)} fusion(s32[4096]{0:T(1024)S(1)} %bitcast.84, s32[4096]{0:T(1024)S(1)} %iota.52, s32[]{:T(128)} %constant.113.clone.1), kind=kCustom, calls=%fused_computation.50 | custom fusion | bytes 49156 | tf_op jit(solution)/shard_map/scatter | solution.py:73
  155.1 39.6 %psum.30 = f32[80,64]{0,1:T(8,128)S(1)} all-reduce(f32[80,64]{0,1:T(8,128)S(1)} %convolution_bitcast_fusion), channel_id=1, replica_groups=mesh['rec'=4,'tract'=8] {'tract'}, use_global_device_ids=true, to_apply=%region_6.7 | all-reduce | flops 5120 | bytes 40960 | tf_op jit(solution)/shard_map/psum | solution.py:57
  194.7 10.4 %psum.31 = f32[80,64]{0,1:T(8,128)S(1)} all-reduce(f32[80,64]{0,1:T(8,128)S(1)} %psum.30), channel_id=1, replica_groups=mesh['rec'=4,'tract'=8] {'rec'}, use_global_device_ids=true, to_apply=%region_7.8 | all-reduce | flops 5120 | bytes 40960 | tf_op jit(solution)/shard_map/psum | solution.py:57
  205.2 48.7 %all-reduce.4.cloned.1.call-done = f32[80,64,64]{1,2,0:T(8,128)} async-done(((f32[80,64,64]{1,2,0:T(8,128)}), f32[80,64,64]{1,2,0:T(8,128)}) %all-reduce.4.cloned.1.call-update) | async-done | bytes 1310736 | tf_op jit(solution)/shard_map/psum | solution.py:57
  254.1 61.2 %all-reduce.6.cloned.1.call-done = f32[80,64,64]{1,2,0:T(8,128)} async-done(((f32[80,64,64]{1,2,0:T(8,128)}), f32[80,64,64]{1,2,0:T(8,128)}) %all-reduce.6.cloned.1.call-update) | async-done | bytes 1310736 | tf_op jit(solution)/shard_map/psum | solution.py:57
  315.3 3.4 copy.21
  318.7 4.1 fusion.9
  322.8 470.6 %custom-call.9 = f32[80,64,64]{2,1,0:T(8,128)} custom-call(f32[80,64,64]{2,1,0:T(8,128)} %fusion.9), custom_call_target="Cholesky" | custom-call | tf_op jit(solution)/shard_map/jit(cholesky)/cholesky | solution.py:24
  793.4 2.7 copy.22
  796.9 1.7 select_bitcast_fusion.1
  798.6 67.2 %custom-call.10 = f32[80,1,64,64]{0,2,3,1:T(8,128)S(1)} custom-call(f32[80,1,64,64]{0,3,2,1:T(8,128)} %select_bitcast_fusion.1), custom_call_target="InvertDiagBlocksLowerTriangular" | custom-call | tf_op jit(solution)/shard_map/triangular_solve | solution.py:27
  866.2 1.0 copy-done.1
  867.3 3.6 copy.33
  870.8 4.2 fusion.23
  875.0 1.8 fusion.22
  877.8 43.3 %gather_fusion = bf16[12288,81]{1,0:T(8,128)(2,1)} fusion(bf16[81,4097]{0,1:T(8,128)(2,1)S(1)} %concatenate.11.clone, s32[12288]{0:T(1024)S(1)} %broadcast_clamp_fusion), kind=kCustom, calls=%fused_computation | custom fusion | bytes 4030464 | tf_op jit(solution)/shard_map/jit(_take)/gather | solution.py:76
  921.2 3.3 copy.26
  924.5 1.6 select_bitcast_fusion
  926.1 5.6 all-to-all-start
  931.8 49.5 %all-to-all-done = bf16[81,8,1536]{2,0,1:T(8,128)(2,1)S(1)} async-done(((bf16[81,8,1536]{2,0,1:T(8,128)(2,1)}), bf16[81,8,1536]{2,0,1:T(8,128)(2,1)S(1)}, u32[]{:S(2)}, u32[]{:S(2)}) %all-to-all-start) | async-done | bytes 1990688 | tf_op jit(solution)/shard_map/all_to_all | solution.py:77
  981.3 29.7 %fusion.10 = f32[2048,80]{0,1:T(8,128)} fusion(f32[8,1536]{1,0:T(8,128)S(1)} %bitcast.82, f32[2048]{0:T(1024)S(1)} %add_multiply_fusion, bf16[81,8,1536]{2,0,1:T(8,128)(2,1)S(1)} %all-to-all-done), kind=kOutput, calls=%fused_computation.16 | convolution fusion | flops 4177526784 | bytes 2678784 | tf_op jit(solution)/shard_map/rsm,smj->jr/dot_general | solution.py:83
  1011.0 21.0 %reduce-scatter.2.cloned.1.call-done = f32[512,80]{0,1:T(8,128)} async-done(((f32[2048,80]{0,1:T(8,128)}), f32[512,80]{0,1:T(8,128)}) %reduce-scatter.2.cloned.1.call-update) | async-done | bytes 163856 | tf_op jit(solution)/shard_map/reduce_scatter | solution.py:82
  1032.0 1.6 multiply_bitcast_fusion
  (82 shorter events, 30.1 us)
Async XLA Ops:
  7.2 246.8 %all-reduce.4.cloned.1.call-start = ((), (), s32[]{:S(2)}) async-start(), calls=%async_computation.2 | async-start | bytes 5242880 | tf_op jit(solution)/shard_map/psum | solution.py:57
  134.8 0.7 copy-start.4
  134.8 19.4 %copy-start.5 = (bf16[4096]{0:T(1024)(128)(2,1)S(1)}, bf16[4096]{0:T(1024)(128)(2,1)}, u32[]{:S(2)}) copy-start(bf16[4096]{0:T(1024)(128)(2,1)} %param.11) | copy-start | bytes 24580
  134.8 19.5 %copy-start.2 = (f32[80,4096]{1,0:T(8,128)S(1)}, f32[80,4096]{1,0:T(8,128)}, u32[]{:S(2)}) copy-start(f32[80,4096]{1,0:T(8,128)} %get-tuple-element.171) | copy-start | bytes 3932164
  134.8 180.5 %all-reduce.6.cloned.1.call-start = ((), (), s32[]{:S(2)}) async-start(), calls=%async_computation.3 | async-start | bytes 5242880 | tf_op jit(solution)/shard_map/psum | solution.py:57
  138.5 115.5 %copy-start.7 = (f32[64]{0:T(128)S(1)}, f32[64]{0:T(128)}, u32[]{:S(2)}) copy-start(f32[64]{0:T(128)} %param.12) | copy-start | bytes 772
  315.3 3.4 copy-start
  865.9 1.4 copy-start.1
  870.8 4.2 copy-start.3
  926.1 5.7 copy-start.6
  926.1 55.2 %all-to-all-start = ((bf16[81,8,1536]{2,0,1:T(8,128)(2,1)}), bf16[81,8,1536]{2,0,1:T(8,128)(2,1)S(1)}, u32[]{:S(2)}, u32[]{:S(2)}) async-start(bf16[81,8,1536]{2,0,1:T(8,128)(2,1)} %select_bitcast_fusion), calls=%async_computation | async-start | bytes 4325376 | tf_op jit(solution)/shard_map/all_to_all | solution.py:77
  931.7 100.3 %reduce-scatter.2.cloned.1.call-start = ((), (), s32[]{:S(2)}) async-start(), calls=%async_computation.4 | async-start | bytes 819200 | tf_op jit(solution)/shard_map/reduce_scatter | solution.py:82
Sparse Core Ops, SparseCore 0:
  135.0 118.9 all-reduce.3
  256.3 58.9 all-reduce.5
  1011.1 20.8 reduce-scatter.1
